TPU v7x, 256 devices: a whole 4x4x8 slice. The times are simulated.
256 devices in a mesh: rows: 32 (over y_lo, z, core), chan: 8 (over x, y_hi).
Axes of the slice: x: 4, y: 4 (y_hi: 2, y_lo: 2; y = y_hi * 2 + y_lo), z: 8, core: 2. Of those that a mesh axis runs over, the one named last changes fastest.
Arguments:
- features: bfloat16 [256, 256, 2048], P('rows', None, 'chan'), may hold values from -6 to 6
- grad_out: bfloat16 [3, 256, 256, 256], P(None, 'rows', 'chan'), may hold values from -6 to 6
- pre_act: bfloat16 [3, 256, 256, 256], P(None, 'rows', 'chan'), may hold values from -6 to 6
- weights: bfloat16 [3, 9, 256, 2048], P(None, None, None, 'chan'), may hold values from -0.046875 to 0.046875
Outputs:
- grad_input: bfloat16 [256, 256, 2048], P('rows', None, 'chan')
- grad_weight: float32 [3, 9, 256, 2048], P(None, None, 'rows', 'chan')
All inputs are finite; a program needn't handle non-finite values.
Results may differ from a plain program's by a relative error of at most 0.001.
Values may be sent and summed in bfloat16 or wider, within the bound.
A program may use at most 128 MiB of HBM per device.

v0:
```python
import jax
import jax.numpy as jnp
from jax import lax
from jax.sharding import PartitionSpec as P

RATE_A = 12
RATE_B = 24
RATE_C = 36


grad_scale = 0.00390625


def passed_along(array, axis, by):
    count = lax.axis_size(axis)
    pairs = [(i, i + by) for i in range(count) if 0 <= i + by < count]
    return lax.ppermute(array, axis, pairs)


def row_plan(rows_dev):
    piece_plan = []
    for branch, dilation in enumerate((RATE_A, RATE_B, RATE_C)):
        for side in (1, -1):
            start_strip = side * dilation // rows_dev
            remainder = side * dilation % rows_dev
            if remainder == 0:
                piece_plan.append((branch, side, start_strip, 0, rows_dev))
            else:
                piece_plan.append((branch, side, start_strip, remainder, rows_dev))
                piece_plan.append((branch, side, start_strip + 1, 0, remainder))
    return piece_plan


def fetch_direct(source, piece_plan):
    received = []
    for entry in piece_plan:
        piece = source[entry[0], entry[3] : entry[4]]
        received.append(passed_along(piece, "rows", -entry[2]))
    return received


def fetch_rows(source, piece_plan):
    received = fetch_direct(source, piece_plan)
    upper_list = []
    lower_list = []
    for branch in range(3):
        for side in (1, -1):
            parts = [
                received[position]
                for position, entry in enumerate(piece_plan)
                if entry[0] == branch and entry[1] == side
            ]
            block = jnp.concatenate(parts, axis=0)
            if side == 1:
                upper_list.append(block)
            else:
                lower_list.append(block)
    return (jnp.stack(upper_list, axis=0), jnp.stack(lower_list, axis=0))


def shards(features, grad_out, pre_act, weights):
    rows_dev = features.shape[0]
    cols = features.shape[1]
    local_chan = features.shape[2]
    out_chan = weights.shape[2]
    piece_plan = row_plan(rows_dev)
    masked = grad_out * (pre_act > 0).astype(jnp.bfloat16)
    own_rows = lax.all_gather(masked, "chan", axis=2, tiled=True)
    upper_rows, lower_rows = fetch_rows(own_rows, piece_plan)
    kernels = weights.reshape(3, 9 * out_chan, local_chan)
    grad_input = jnp.zeros((rows_dev, cols, local_chan), jnp.float32)
    kernel_list = []
    for branch, dilation in enumerate((RATE_A, RATE_B, RATE_C)):
        rows_by_step = {-1: upper_rows[branch], 0: own_rows[branch], 1: lower_rows[branch]}
        tap_list = []
        for row_step in (-1, 0, 1):
            padded = jnp.pad(rows_by_step[row_step], ((0, 0), (0, 0), (dilation, dilation)))
            for col_step in (-1, 0, 1):
                cols_at = dilation - col_step * dilation
                tap_list.append(padded[:, :, cols_at : cols_at + cols])
        stacked_taps = jnp.concatenate(tap_list, axis=1)
        grad_input = grad_input + jnp.einsum(
            "rkc,ki->rci", stacked_taps, kernels[branch], preferred_element_type=jnp.float32
        )
        kernel_list.append(
            jnp.einsum("rkc,rci->ki", stacked_taps, features, preferred_element_type=jnp.float32)
        )
    partial_grad = jnp.stack(kernel_list, axis=0).reshape(3, 9, out_chan, local_chan)
    summed = lax.psum_scatter(partial_grad, "rows", scatter_dimension=2, tiled=True)
    return (grad_input.astype(jnp.bfloat16), summed * grad_scale)


def solution(mesh):
    in_specs = (
        P("rows", None, "chan"),
        P(None, "rows", "chan", None),
        P(None, "rows", "chan", None),
        P(None, None, None, "chan"),
    )
    out_specs = (P("rows", None, "chan"), P(None, None, "rows", "chan"))
    return jax.shard_map(shards, mesh=mesh, in_specs=in_specs, out_specs=out_specs, check_vma=False)
```

profile of v0, /device:TPU:32, one launch (start us, length us, event | category | flops | bytes accessed | tf_op | source)
XLA Modules:
  0.0 341.7 jit_solution(2801595185410041347)
XLA Ops:
  7.2 2.4 compare_select_fusion
  9.7 72.3 %all-gather.2.cloned.1.call-done = bf16[3,8,256,256]{3,1,0,2:T(8,128)(2,1)} async-done(((bf16[3,8,32,256]{3,1,0,2:T(8,128)(2,1)}), bf16[3,8,256,256]{3,1,0,2:T(8,128)(2,1)}) %all-gather.2.cloned.1.call-update) | async-done | bytes 3145744 | tf_op jit(solution)/shard_map/all_gather | solution.py:68
  82.0 3.1 fusion.20
  85.1 1.2 copy.31
  86.3 1.2 copy.30
  87.5 1.3 collective-permute-start.6
  88.7 1.3 collective-permute-start.7
  90.0 1.1 copy.27
  91.2 1.9 collective-permute-start.3
  93.1 2.6 collective-permute-start.1
  95.7 8.7 %collective-permute-start.8 = (bf16[4,256,256]{1,2,0:T(8,128)(2,1)}, bf16[4,256,256]{1,2,0:T(8,128)(2,1)}, u32[]{:S(2)}, u32[]{:S(2)}) collective-permute-start(bf16[4,256,256]{1,2,0:T(8,128)(2,1)} %bitcast.8), channel_id=1, source_target_pairs={{0,40},{8,48},{16,56},{24,64},{32,72},{40,80},{48,88},{56,96},{64,... | collective-permute-start | bytes 1572872 | tf_op jit(solution)/shard_map/ppermute | solution.py:17
  104.4 1.1 copy.26
  105.5 3.4 %fusion.19 = (bf16[1,8,256,256]{3,1,0,2:T(8,128)(2,1)S(1)}, bf16[1,8,256,256]{3,1,0,2:T(8,128)(2,1)}, bf16[1,8,256,256]{3,1,0,2:T(8,128)(2,1)}) fusion(bf16[3,8,256,256]{3,1,0,2:T(8,128)(2,1)} %all-gather.2.cloned.1.call-done), kind=kLoop, calls=%fused_computation.60 | loop fusion | bytes 6291456 | tf_op jit(solution)/shard_map/slice | solution.py:37
  108.9 0.8 copy.29
  109.7 1.6 copy.28
  111.4 2.4 copy.32
  113.8 4.0 %collective-permute-start.9 = (bf16[4,256,256]{1,2,0:T(8,128)(2,1)}, bf16[4,256,256]{1,2,0:T(8,128)(2,1)S(1)}, u32[]{:S(2)}, u32[]{:S(2)}) collective-permute-start(bf16[4,256,256]{1,2,0:T(8,128)(2,1)} %bitcast.57), channel_id=1, source_target_pairs={{0,32},{8,40},{16,48},{24,56},{32,64},{40,72},{48,80},{56,88},{64,... | collective-permute-start | bytes 1572872 | tf_op jit(solution)/shard_map/ppermute | solution.py:17
  117.8 19.8 %collective-permute-done.7 = bf16[4,256,256]{1,2,0:T(8,128)(2,1)} collective-permute-done((bf16[4,256,256]{1,2,0:T(8,128)(2,1)}, bf16[4,256,256]{1,2,0:T(8,128)(2,1)}, u32[]{:S(2)}, u32[]{:S(2)}) %collective-permute-start.7) | collective-permute-done | bytes 524320 | tf_op jit(solution)/shard_map/ppermute | solution.py:17
  137.6 2.3 collective-permute-start.2
  139.9 1.5 fusion.4
  141.4 1.1 constant_dynamic-update-slice_fusion.12
  142.5 1.1 constant_dynamic-update-slice_fusion.11
  143.6 0.1 slice_dynamic-update-slice_fusion.2
  143.7 0.2 fusion.16
  143.9 0.1 constant_dynamic-update-slice_fusion.10
  144.0 0.2 fusion.17
  144.2 10.5 %collective-permute-start = (bf16[4,256,256]{1,2,0:T(8,128)(2,1)S(1)}, bf16[4,256,256]{1,2,0:T(8,128)(2,1)S(1)}, u32[]{:S(2)}, u32[]{:S(2)}) collective-permute-start(bf16[4,256,256]{1,2,0:T(8,128)(2,1)S(1)} %bitcast.55), channel_id=1, source_target_pairs={{8,0},{16,8},{24,16},{32,24},{40,32},{48,40},{56,48},{64,56},{72,6... | collective-permute-start | bytes 1572872 | tf_op jit(solution)/shard_map/ppermute | solution.py:17
  154.7 3.4 collective-permute-start.5
  158.1 1.3 select_maximum_fusion
  159.5 0.1 slice_dynamic-update-slice_fusion.1
  159.5 1.1 constant_dynamic-update-slice_fusion.9
  160.7 0.1 slice_dynamic-update-slice_fusion
  160.8 1.5 collective-permute-start.4
  162.2 1.7 fusion.7
  164.1 1.1 constant_dynamic-update-slice_fusion.3
  165.2 0.1 slice_dynamic-update-slice_fusion.6
  165.2 0.2 fusion.8
  165.5 0.1 constant_dynamic-update-slice_fusion.2
  165.6 0.2 fusion.9
  165.8 2.8 fusion.25
  168.6 1.3 select_maximum_fusion.1
  170.0 0.1 slice_dynamic-update-slice_fusion.5
  170.1 1.1 constant_dynamic-update-slice_fusion
  171.2 0.1 slice_dynamic-update-slice_fusion.4
  171.3 2.8 fusion.23
  174.1 0.8 copy-done.4
  174.9 27.4 %collective-permute-done.4 = bf16[8,256,256]{1,2,0:T(8,128)(2,1)S(1)} collective-permute-done((bf16[8,256,256]{1,2,0:T(8,128)(2,1)S(1)}, bf16[8,256,256]{1,2,0:T(8,128)(2,1)S(1)}, u32[]{:S(2)}, u32[]{:S(2)}) %collective-permute-start.4) | collective-permute-done | bytes 1048608 | tf_op jit(solution)/shard_map/ppermute | solution.py:17
  202.2 0.1 fusion.10
  202.3 0.1 constant_dynamic-update-slice_fusion.7
  202.4 0.1 fusion.11
  202.5 0.1 fusion.12
  202.6 0.1 constant_dynamic-update-slice_fusion.6
  202.6 0.1 fusion.13
  202.7 0.1 fusion.14
  202.9 0.1 fusion.15
  203.0 2.8 fusion.24
  205.8 0.8 copy-done.5
  206.6 3.3 pad_maximum_fusion
  210.0 2.4 fusion.18
  212.4 5.7 %fusion.21 = f32[8,256,256]{2,1,0:T(8,128)S(1)} fusion(bf16[8,2304,256]{1,2,0:T(8,128)(2,1)} %copy-done.4, bf16[2304,256,1]{1,0,2:T(8,128)(2,1)S(1)} %bitcast.53), kind=kOutput, calls=%fused_computation.62 | convolution fusion | flops 2415919104 | bytes 12713984 | tf_op jit(solution)/shard_map/rkc,ki->rci/dot_general | solution.py:82
  218.2 2.7 fusion.22
  221.0 3.8 %add_convert_fusion = bf16[8,256,256]{2,1,0:T(8,128)(2,1)} fusion(f32[8,256,256]{2,1,0:T(8,128)S(1)} %fusion.21, f32[8,256,256]{2,1,0:T(8,128)S(1)} %fusion.22, bf16[8,2304,256]{1,2,0:T(8,128)(2,1)S(1)} %bitcast.59, bf16[2304,256,1]{1,0,2:T(8,128)(2,1)S(1)} %bitcast.51), kind=kOutput, calls=%fused_computation.7 | convolution fusion | flops 2417491968 | bytes 15859712 | tf_op jit(solution)/shard_map/rkc,ki->rci/dot_general | solution.py:82
  224.8 108.4 %reduce-scatter.2.cloned.1.call-done = f32[3,9,8,256]{3,2,1,0:T(8,128)} async-done(((f32[3,9,256,256]{3,2,1,0:T(8,128)}), f32[3,9,8,256]{3,2,1,0:T(8,128)}) %reduce-scatter.2.cloned.1.call-update) | async-done | bytes 221200 | tf_op jit(solution)/shard_map/reduce_scatter | solution.py:89
  333.2 1.6 broadcast_multiply_fusion
  (42 shorter events, 0.5 us)
Async XLA Ops:
  7.2 158.6 %copy-start = (bf16[8,256,256]{2,1,0:T(8,128)(2,1)S(1)}, bf16[8,256,256]{2,1,0:T(8,128)(2,1)}, u32[]{:S(2)}) copy-start(bf16[8,256,256]{2,1,0:T(8,128)(2,1)} %param.4) | copy-start | bytes 3145732
  7.2 74.8 %all-gather.2.cloned.1.call-start = ((), (), s32[]{:S(2)}) async-start(), calls=%async_computation.1 | async-start | bytes 3538944 | tf_op jit(solution)/shard_map/all_gather | solution.py:68
  9.6 323.6 %reduce-scatter.2.cloned.1.call-start = ((), (), s32[]{:S(2)}) async-start(), calls=%async_computation.2 | async-start | bytes 7299072 | tf_op jit(solution)/shard_map/reduce_scatter | solution.py:89
  87.5 26.3 %collective-permute-start.6 = (bf16[4,256,256]{1,2,0:T(8,128)(2,1)}, bf16[4,256,256]{1,2,0:T(8,128)(2,1)}, u32[]{:S(2)}, u32[]{:S(2)}) collective-permute-start(bf16[4,256,256]{1,2,0:T(8,128)(2,1)} %bitcast.8), channel_id=1, source_target_pairs={{32,0},{40,8},{48,16},{56,24},{64,32},{72,40},{80,48},{88,56},{96,... | collective-permute-start | bytes 1572872 | tf_op jit(solution)/shard_map/ppermute | solution.py:17
  88.7 48.8 %collective-permute-start.7 = (bf16[4,256,256]{1,2,0:T(8,128)(2,1)}, bf16[4,256,256]{1,2,0:T(8,128)(2,1)}, u32[]{:S(2)}, u32[]{:S(2)}) collective-permute-start(bf16[4,256,256]{1,2,0:T(8,128)(2,1)} %bitcast.56), channel_id=1, source_target_pairs={{40,0},{48,8},{56,16},{64,24},{72,32},{80,40},{88,48},{96,56},{104... | collective-permute-start | bytes 1572872 | tf_op jit(solution)/shard_map/ppermute | solution.py:17
  91.2 77.4 %collective-permute-start.3 = (bf16[4,256,256]{1,2,0:T(8,128)(2,1)}, bf16[4,256,256]{1,2,0:T(8,128)(2,1)}, u32[]{:S(2)}, u32[]{:S(2)}) collective-permute-start(bf16[4,256,256]{1,2,0:T(8,128)(2,1)} %bitcast.1), channel_id=1, source_target_pairs={{0,8},{8,16},{16,24},{24,32},{32,40},{40,48},{48,56},{56,64},{64,7... | collective-permute-start | bytes 1572872 | tf_op jit(solution)/shard_map/ppermute | solution.py:17
  93.1 67.6 %collective-permute-start.1 = (bf16[4,256,256]{1,2,0:T(8,128)(2,1)}, bf16[4,256,256]{1,2,0:T(8,128)(2,1)}, u32[]{:S(2)}, u32[]{:S(2)}) collective-permute-start(bf16[4,256,256]{1,2,0:T(8,128)(2,1)} %bitcast.1), channel_id=1, source_target_pairs={{16,0},{24,8},{32,16},{40,24},{48,32},{56,40},{64,48},{72,56},{80,... | collective-permute-start | bytes 1572872 | tf_op jit(solution)/shard_map/ppermute | solution.py:17
  95.7 48.5 %collective-permute-start.8 = (bf16[4,256,256]{1,2,0:T(8,128)(2,1)}, bf16[4,256,256]{1,2,0:T(8,128)(2,1)}, u32[]{:S(2)}, u32[]{:S(2)}) collective-permute-start(bf16[4,256,256]{1,2,0:T(8,128)(2,1)} %bitcast.8), channel_id=1, source_target_pairs={{0,40},{8,48},{16,56},{24,64},{32,72},{40,80},{48,88},{56,96},{64,... | collective-permute-start | bytes 1572872 | tf_op jit(solution)/shard_map/ppermute | solution.py:17
  113.8 29.9 %copy-start.1 = (bf16[1,8,256,256]{2,3,1,0:T(8,128)(2,1)S(1)}, bf16[1,8,256,256]{2,3,1,0:T(8,128)(2,1)}, u32[]{:S(2)}) copy-start(bf16[1,8,256,256]{2,3,1,0:T(8,128)(2,1)} %copy.32) | copy-start | bytes 3145732
  113.8 40.9 %collective-permute-start.9 = (bf16[4,256,256]{1,2,0:T(8,128)(2,1)}, bf16[4,256,256]{1,2,0:T(8,128)(2,1)S(1)}, u32[]{:S(2)}, u32[]{:S(2)}) collective-permute-start(bf16[4,256,256]{1,2,0:T(8,128)(2,1)} %bitcast.57), channel_id=1, source_target_pairs={{0,32},{8,40},{16,48},{24,56},{32,64},{40,72},{48,80},{56,88},{64,... | collective-permute-start | bytes 1572872 | tf_op jit(solution)/shard_map/ppermute | solution.py:17
  137.6 6.7 %copy-start.2 = (bf16[1,4,256,256]{2,3,1,0:T(8,128)(2,1)S(1)}, bf16[1,4,256,256]{2,3,1,0:T(8,128)(2,1)}, u32[]{:S(2)}) copy-start(bf16[1,4,256,256]{2,3,1,0:T(8,128)(2,1)} %copy.26) | copy-start | bytes 1572868
  137.6 31.1 %collective-permute-start.2 = (bf16[4,256,256]{1,2,0:T(8,128)(2,1)}, bf16[4,256,256]{1,2,0:T(8,128)(2,1)S(1)}, u32[]{:S(2)}, u32[]{:S(2)}) collective-permute-start(bf16[4,256,256]{1,2,0:T(8,128)(2,1)} %bitcast.54), channel_id=1, source_target_pairs={{0,16},{8,24},{16,32},{24,40},{32,48},{40,56},{48,64},{56,72},{64,... | collective-permute-start | bytes 1572872 | tf_op jit(solution)/shard_map/ppermute | solution.py:17
  144.2 18.0 %collective-permute-start = (bf16[4,256,256]{1,2,0:T(8,128)(2,1)S(1)}, bf16[4,256,256]{1,2,0:T(8,128)(2,1)S(1)}, u32[]{:S(2)}, u32[]{:S(2)}) collective-permute-start(bf16[4,256,256]{1,2,0:T(8,128)(2,1)S(1)} %bitcast.55), channel_id=1, source_target_pairs={{8,0},{16,8},{24,16},{32,24},{40,32},{48,40},{56,48},{64,56},{72,6... | collective-permute-start | bytes 1572872 | tf_op jit(solution)/shard_map/ppermute | solution.py:17
  154.7 48.0 %collective-permute-start.5 = (bf16[8,256,256]{1,2,0:T(8,128)(2,1)S(1)}, bf16[8,256,256]{1,2,0:T(8,128)(2,1)S(1)}, u32[]{:S(2)}, u32[]{:S(2)}) collective-permute-start(bf16[8,256,256]{1,2,0:T(8,128)(2,1)S(1)} %bitcast.40), channel_id=1, source_target_pairs={{0,24},{8,32},{16,40},{24,48},{32,56},{40,64},{48,72},{56,80},{64,... | collective-permute-start | bytes 3145736 | tf_op jit(solution)/shard_map/ppermute | solution.py:17
  160.7 5.1 %copy-start.3 = (bf16[8,2304,256]{1,2,0:T(8,128)(2,1)}, bf16[8,2304,256]{1,2,0:T(8,128)(2,1)S(1)}, u32[]{:S(2)}) copy-start(bf16[8,2304,256]{1,2,0:T(8,128)(2,1)S(1)} %slice_dynamic-update-slice_fusion) | copy-start | bytes 28311556
  160.8 41.5 %collective-permute-start.4 = (bf16[8,256,256]{1,2,0:T(8,128)(2,1)S(1)}, bf16[8,256,256]{1,2,0:T(8,128)(2,1)S(1)}, u32[]{:S(2)}, u32[]{:S(2)}) collective-permute-start(bf16[8,256,256]{1,2,0:T(8,128)(2,1)S(1)} %bitcast.41), channel_id=1, source_target_pairs={{24,0},{32,8},{40,16},{48,24},{56,32},{64,40},{72,48},{80,56},{88,... | collective-permute-start | bytes 3145736 | tf_op jit(solution)/shard_map/ppermute | solution.py:17
  171.2 3.6 %copy-start.4 = (bf16[8,2304,256]{1,2,0:T(8,128)(2,1)}, bf16[8,2304,256]{1,2,0:T(8,128)(2,1)S(1)}, u32[]{:S(2)}) copy-start(bf16[8,2304,256]{1,2,0:T(8,128)(2,1)S(1)} %slice_dynamic-update-slice_fusion.4) | copy-start | bytes 28311556
  203.0 3.7 %copy-start.5 = (bf16[8,2304,256]{1,2,0:T(8,128)(2,1)}, bf16[8,2304,256]{1,2,0:T(8,128)(2,1)S(1)}, u32[]{:S(2)}) copy-start(bf16[8,2304,256]{1,2,0:T(8,128)(2,1)S(1)} %fusion.15) | copy-start | bytes 28311556
  210.0 8.2 %slice-start.3 = ((s8[9437184]{0:T(1024)(128)(4,1)}), s8[1048576]{0:T(1024)(128)(4,1)S(1)}, s32[]{:S(2)}) async-start(s8[9437184]{0:T(1024)(128)(4,1)} %bitcast.60), calls=%async_computation.6 | async-start | bytes 2097152
  210.0 8.2 %slice-start.4 = ((s8[9437184]{0:T(1024)(128)(4,1)}), s8[4194304]{0:T(1024)(128)(4,1)S(1)}, s32[]{:S(2)}) async-start(s8[9437184]{0:T(1024)(128)(4,1)} %bitcast.60), calls=%async_computation.7 | async-start | bytes 8388608
  212.4 5.8 %slice-start.5 = ((s8[9437184]{0:T(1024)(128)(4,1)}), s8[4194304]{0:T(1024)(128)(4,1)S(1)}, s32[]{:S(2)}) async-start(s8[9437184]{0:T(1024)(128)(4,1)} %bitcast.60), calls=%async_computation.8 | async-start | bytes 8388608
  212.4 8.5 %slice-start = ((s8[9437184]{0:T(1024)(128)(4,1)}), s8[4194304]{0:T(1024)(128)(4,1)S(1)}, s32[]{:S(2)}) async-start(s8[9437184]{0:T(1024)(128)(4,1)} %bitcast.58), calls=%async_computation.3 | async-start | bytes 8388608
  212.4 8.5 %slice-start.1 = ((s8[9437184]{0:T(1024)(128)(4,1)}), s8[4194304]{0:T(1024)(128)(4,1)S(1)}, s32[]{:S(2)}) async-start(s8[9437184]{0:T(1024)(128)(4,1)} %bitcast.58), calls=%async_computation.4 | async-start | bytes 8388608
  218.2 2.8 slice-start.2
Sparse Core Ops, SparseCore 0:
  11.2 70.7 all-gather.1
  210.1 123.0 reduce-scatter.1
where the time goes:
time: 347 us; the launch traced here: 342 us
  waiting for transfers between devices  228 us (66%)
  starting transfers between devices  37.4 us (11%)
  local copies, waits for them, and re-layouts  27.8 us (8%)
  matrix products  20.7 us (6%)
  between operations  14.6 us (4%)
  other arithmetic  13.2 us (4%)
    reduce_scatter x1, waiting for transfers between devices, shards(): lax.psum_scatter(partial_grad, 'rows', scatter_dimension=2, tiled=True)  108 us
    all_gather x1, waiting for transfers between devices, shards(): own_rows = lax.all_gather(masked, 'chan', axis=2, tiled=True)  72.3 us
    ppermute x10, waiting for transfers between devices, passed_along(): return lax.ppermute(array, axis, pairs)  47.2 us
    ppermute x10, starting transfers between devices, passed_along(): return lax.ppermute(array, axis, pairs)  37.4 us
    unnamed x59, local copies, waits for them, and re-layouts  18.7 us
    dot_general x3, matrix products, shards(): jnp.einsum('rkc,ki->rci', stacked_taps, kernels[branch], preferred_elemen...  12.3 us
    dot_general x3, matrix products, shards(): jnp.einsum('rkc,rci->ki', stacked_taps, features, preferred_element_type=...  8.4 us
  transfers between devices with their start and end apart: 12, of which 4 were waited for; matrix products, arithmetic and copies ran while one was open for 13% of the time, Pallas kernels for 0%

commit v1 on v0

v1 whole, which is shorter than its diff:
```python
import jax
import jax.numpy as jnp
from jax import lax
from jax.experimental import pallas as pl
from jax.experimental.pallas import tpu as pltpu
from jax.sharding import PartitionSpec as P

RATES = (12, 24, 36)
MESH = pl.DeviceIdType.MESH
BF16 = jnp.bfloat16
F32 = jnp.float32

grad_scale = 0.00390625

PIECES = ((0, 0), (1, 0), (2, 0), (0, -1), (0, 1), (1, -1), (1, 1), (2, -1), (2, 1))
RING = (0, 1, 2, 5, 6, 7, 8)
DIRECT = (3, 4)

STRIP = 8
COLS = 256
UNIT = 32


def row_parts():
    parts = []
    for p, (b, i) in enumerate(PIECES):
        if i == 0:
            continue
        start = -i * RATES[b]
        offset, first = start // STRIP, start % STRIP
        if first == 0:
            parts.append((p, offset, 0, 0, STRIP))
        else:
            parts.append((p, offset, first, 0, STRIP - first))
            parts.append((p, offset + 1, 0, STRIP - first, first))
    return parts


PARTS = row_parts()


def kernel(
    feat, gout, pre, w, gin, gw,
    g, m3, wt, acc, part, r0, qs, ry, sz, rz,
    h_send, h_recv, y_send, y_recv, x_send, x_recv, f_send, f_recv,
    c_send, c_recv, v_send, v_recv, z_send, z_recv,
):
    s = lax.axis_index("rows")
    k = lax.axis_index("chan")
    core = lax.rem(s, 2)
    zpos = lax.rem(s // 2, 8)
    yl = s // 16
    yh = lax.rem(k, 2)
    k_even = k - yh
    k_pair = k + 1 - 2 * yh
    k_left = lax.rem(k + 6, 8)
    k_right = lax.rem(k + 2, 8)

    barrier = pltpu.get_barrier_semaphore()

    @pl.loop(1, 32)
    def _(d):
        pl.semaphore_signal(barrier, inc=1, device_id=(lax.rem(s + d, 32), k), device_id_type=MESH)

    for peer in (k_pair, k_left, k_right):
        pl.semaphore_signal(barrier, inc=1, device_id=(s, peer), device_id_type=MESH)

    own = pl.ds(pl.multiple_of(k * UNIT, UNIT), UNIT)
    for b in range(3):
        for y in range(STRIP):
            value = gout[b, y] * (pre[b, y] > 0).astype(BF16)
            g[b, own, y * COLS : (y + 1) * COLS] = value

    for p, offset, _, here, rows in PARTS:
        @pl.when((s + offset < 0) | (s + offset > 31))
        def _(p=p, here=here, rows=rows):
            cols = slice(here * COLS, (here + rows) * COLS)
            if p in DIRECT:
                g[p, :, cols] = jnp.zeros((256, rows * COLS), BF16)
            else:
                g[p, own, cols] = jnp.zeros((UNIT, rows * COLS), BF16)

    pl.semaphore_wait(barrier, 34)

    def halo_copy(n):
        p, offset, there, here, rows = PARTS[n]
        b = PIECES[p][0]
        take = slice(None) if p in DIRECT else own
        return pltpu.make_async_remote_copy(
            src_ref=g.at[b, take, there * COLS : (there + rows) * COLS],
            dst_ref=g.at[p, take, here * COLS : (here + rows) * COLS],
            send_sem=h_send.at[n], recv_sem=h_recv.at[n],
            device_id=(jnp.clip(s - offset, 0, 31), k), device_id_type=MESH,
        )

    def halo_sends(p):
        for n, entry in enumerate(PARTS):
            if entry[0] == p:
                @pl.when((s - entry[1] >= 0) & (s - entry[1] <= 31))
                def _(n=n):
                    halo_copy(n).start()

    def halo_waits(p):
        for n, entry in enumerate(PARTS):
            if entry[0] == p:
                @pl.when((s + entry[1] >= 0) & (s + entry[1] <= 31))
                def _(n=n):
                    halo_copy(n).wait_recv()

    def halo_drain(p):
        for n, entry in enumerate(PARTS):
            if entry[0] == p:
                @pl.when((s - entry[1] >= 0) & (s - entry[1] <= 31))
                def _(n=n):
                    halo_copy(n).wait_send()

    def remote(src, dst, send, recv, target):
        return pltpu.make_async_remote_copy(
            src_ref=src, dst_ref=dst, send_sem=send, recv_sem=recv, device_id=target, device_id_type=MESH
        )

    def y_copy(p):
        return remote(g.at[p, own], g.at[p, own], y_send.at[p], y_recv.at[p], (s, k_pair))

    def pair_rows(first, count=2 * UNIT):
        return pl.ds(pl.multiple_of(first * UNIT, UNIT), count)

    def x_copies(p):
        rows = pair_rows(k_even)
        return (
            remote(g.at[p, rows], g.at[p, rows], x_send.at[p, 0], x_recv.at[p, 0], (s, k_right)),
            remote(g.at[p, rows], g.at[p, rows], x_send.at[p, 1], x_recv.at[p, 1], (s, k_left)),
        )

    def f_copies(p):
        from_left = pair_rows(lax.rem(k_even + 6, 8), UNIT)
        from_right = pair_rows(lax.rem(k_even + 2, 8) + 1, UNIT)
        return (
            remote(g.at[p, from_left], g.at[p, from_left], f_send.at[p, 0], f_recv.at[p, 0], (s, k_right)),
            remote(g.at[p, from_right], g.at[p, from_right], f_send.at[p, 1], f_recv.at[p, 1], (s, k_left)),
        )

    def stage_y(p):
        if PIECES[p][1] != 0:
            halo_waits(p)
        y_copy(p).start()

    def stage_x(p):
        y_copy(p).wait_recv()
        for copy in x_copies(p):
            copy.start()

    def stage_f(p):
        for copy in x_copies(p):
            copy.wait_recv()
        for copy in f_copies(p):
            copy.start()

    def stage_ready(p):
        if p in DIRECT:
            halo_waits(p)
        else:
            for copy in f_copies(p):
                copy.wait_recv()

    def transpose_kernels(p):
        b, i = PIECES[p]
        for j in range(3):
            wt[p, :, j * 256 : (j + 1) * 256] = w[b, (i + 1) * 3 + j].T

    def c_copy(p):
        return remote(part.at[p, :, :, :, 1 - core], r0.at[p], c_send.at[p], c_recv.at[p], (s + 1 - 2 * core, k))

    def v_copy(p):
        return remote(qs.at[p], ry.at[p], v_send.at[p], v_recv.at[p], (lax.rem(s + 16, 32), k))

    def z_copy(p, d):
        z_to = lax.rem(zpos + d, 8)
        return remote(
            sz.at[p, z_to], rz.at[p, d - 1], z_send.at[p], z_recv.at[p], (yl * 16 + z_to * 2 + core, k)
        )

    def z_whole(p):
        return remote(sz.at[p, 0:7], rz.at[p], z_send.at[p], z_recv.at[p], (lax.rem(s + 2, 32), k))

    def compute(p, first):
        b, i = PIECES[p]
        rate = RATES[b]

        @pl.loop(0, STRIP)
        def _(y):
            cols = pl.ds(pl.multiple_of(y * COLS, COLS), COLS)
            value = g[p, :, cols]
            edge = jnp.zeros((256, rate), BF16)
            m3[0:256, cols] = jnp.concatenate([value[:, rate:], edge], axis=1)
            m3[256:512, cols] = value
            m3[512:768, cols] = jnp.concatenate([edge, value[:, : COLS - rate]], axis=1)

        @pl.loop(0, 3)
        def _(j):
            rows = pl.ds(pl.multiple_of(j * 256, 256), 256)
            product = jnp.dot(m3[rows, :], feat[...], preferred_element_type=F32)
            part[p, j] = product.reshape(2, 8, 2, 8, 256)

        c_copy(p).start()

        @pl.loop(0, STRIP)
        def _(y):
            cols = pl.ds(pl.multiple_of(y * COLS, COLS), COLS)
            product = jnp.dot(wt[p], m3[:, cols], preferred_element_type=F32)
            if first:
                acc[:, cols] = product
            else:
                acc[:, cols] += product

    def reduce_core(p):
        c_copy(p).wait_recv()
        for j in range(3):
            qs[p, j] = part[p, j, 1 - yl, :, core] + r0[p, j, 1 - yl]
        v_copy(p).start()

    def reduce_y(p):
        v_copy(p).wait_recv()
        for j in range(3):
            sz[p, :, j] = part[p, j, yl, :, core] + r0[p, j, yl] + ry[p, j]
        for d in range(1, 8):
            z_copy(p, d).start()

    def reduce_z(p):
        b, i = PIECES[p]
        z_whole(p).wait_recv()
        total = sz[p, zpos]
        for d in range(7):
            total = total + rz[p, d]
        gw[b, 3 * (i + 1) : 3 * (i + 1) + 3] = total * grad_scale

    stage_y(0)
    for p in (1, 2):
        stage_y(p)
    for p in (5, 6, 7, 8):
        halo_sends(p)
    stage_x(0)
    transpose_kernels(0)
    stage_x(1)
    stage_f(0)
    stage_y(5)
    stage_x(2)
    transpose_kernels(1)
    stage_ready(0)
    for p in DIRECT:
        halo_sends(p)
    stage_f(1)
    stage_y(6)
    compute(0, True)
    stage_x(5)
    transpose_kernels(2)
    stage_ready(1)
    stage_f(2)
    stage_y(7)
    compute(1, False)
    reduce_core(0)
    stage_x(6)
    transpose_kernels(3)
    stage_ready(2)
    stage_f(5)
    stage_y(8)
    compute(2, False)
    reduce_core(1)
    reduce_y(0)
    stage_x(7)
    transpose_kernels(5)
    stage_ready(5)
    stage_f(6)
    compute(5, False)
    reduce_core(2)
    reduce_y(1)
    stage_x(8)
    transpose_kernels(4)
    stage_ready(3)
    compute(3, False)
    reduce_core(5)
    reduce_y(2)
    transpose_kernels(6)
    stage_ready(6)
    stage_f(7)
    compute(6, False)
    reduce_core(3)
    reduce_y(5)
    stage_ready(4)
    compute(4, False)
    reduce_core(6)
    reduce_y(3)
    transpose_kernels(7)
    transpose_kernels(8)
    reduce_z(0)
    stage_ready(7)
    stage_f(8)
    compute(7, False)
    reduce_core(4)
    reduce_y(6)
    reduce_z(1)
    reduce_z(2)
    reduce_core(7)
    reduce_y(4)
    stage_ready(8)
    compute(8, False)
    reduce_y(7)
    reduce_core(8)

    @pl.loop(0, STRIP)
    def _(y):
        cols = pl.ds(pl.multiple_of(y * COLS, COLS), COLS)
        gin[y] = acc[:, cols].astype(BF16).T

    reduce_y(8)
    for p in (5, 3, 6, 4, 7, 8):
        reduce_z(p)

    for p in range(9):
        if PIECES[p][1] != 0:
            halo_drain(p)
        if p in RING:
            y_copy(p).wait_send()
            for copy in x_copies(p):
                copy.wait_send()
            for copy in f_copies(p):
                copy.wait_send()
        c_copy(p).wait_send()
        v_copy(p).wait_send()
        z_whole(p).wait_send()


def shards(features, grad_out, pre_act, weights):
    dma = pltpu.SemaphoreType.DMA
    vmem = pl.BlockSpec(memory_space=pltpu.VMEM)
    return pl.pallas_call(
        kernel,
        out_shape=(
            jax.ShapeDtypeStruct((8, 256, 256), BF16),
            jax.ShapeDtypeStruct((3, 9, 8, 256), F32),
        ),
        in_specs=[vmem] * 4,
        out_specs=(vmem, vmem),
        scratch_shapes=[
            pltpu.VMEM((9, 256, 2048), BF16),
            pltpu.VMEM((768, 2048), BF16),
            pltpu.VMEM((9, 256, 768), BF16),
            pltpu.VMEM((256, 2048), F32),
            pltpu.VMEM((9, 3, 2, 8, 2, 8, 256), F32),
            pltpu.VMEM((9, 3, 2, 8, 8, 256), F32),
            pltpu.VMEM((9, 3, 8, 8, 256), F32),
            pltpu.VMEM((9, 3, 8, 8, 256), F32),
            pltpu.VMEM((9, 8, 3, 8, 256), F32),
            pltpu.VMEM((9, 7, 3, 8, 256), F32),
            dma((len(PARTS),)), dma((len(PARTS),)),
            dma((9,)), dma((9,)),
            dma((9, 2)), dma((9, 2)),
            dma((9, 2)), dma((9, 2)),
            dma((9,)), dma((9,)),
            dma((9,)), dma((9,)),
            dma((9,)), dma((9,)),
        ],
        compiler_params=pltpu.CompilerParams(
            collective_id=0, has_side_effects=True, vmem_limit_bytes=62 * 2**20
        ),
        cost_estimate=pl.CostEstimate(flops=14495514624, bytes_accessed=8 * 2**20, transcendentals=0),
    )(features.reshape(2048, 256), grad_out, pre_act, weights)


def solution(mesh):
    in_specs = (
        P("rows", None, "chan"),
        P(None, "rows", "chan", None),
        P(None, "rows", "chan", None),
        P(None, None, None, "chan"),
    )
    out_specs = (P("rows", None, "chan"), P(None, None, "rows", "chan"))
    return jax.shard_map(shards, mesh=mesh, in_specs=in_specs, out_specs=out_specs, check_vma=False)
```

time: 347 us -> 121 us (0.35); the launches traced: 342 us -> 120 us
  waiting for transfers between devices: 228 us -> 0 us
  Pallas kernels: 0 us -> 116 us
  starting transfers between devices: 37.4 us -> 0 us
  local copies, waits for them, and re-layouts: 27.8 us -> 3.9 us
  matrix products: 20.7 us -> 0 us
  between operations: 14.6 us -> 0.64 us
  other arithmetic: 13.2 us -> 0 us
    pallas_call x0 -> x1, Pallas kernels: none -> 116 us  [shards(): pl.pallas_call(kernel, out_shape=(jax.ShapeDtypeStruct((8, 256, 256), BF1...]
    reduce_scatter x1 -> x0, waiting for transfers between devices: 108 us -> none  [shards(): lax.psum_scatter(partial_grad, 'rows', scatter_dimension=2, tiled=True)]
    all_gather x1 -> x0, waiting for transfers between devices: 72.3 us -> none  [shards(): own_rows = lax.all_gather(masked, 'chan', axis=2, tiled=True)]
    ppermute x10 -> x0, waiting for transfers between devices: 47.2 us -> none  [passed_along(): return lax.ppermute(array, axis, pairs)]
    ppermute x10 -> x0, starting transfers between devices: 37.4 us -> none  [passed_along(): return lax.ppermute(array, axis, pairs)]
    dot_general x6 -> x0, matrix products: 20.7 us -> none  [the longest x3 12.3 us: shards(): jnp.einsum('rkc,ki->rci', stacked_taps, kernels[branch], preferred_elemen...]
    unnamed x59 -> x2, local copies, waits for them, and re-layouts: 18.7 us -> 3.9 us
    slice x3 -> x0, local copies, waits for them, and re-layouts: 8.93 us -> none  [the longest x2 6.55 us: fetch_direct(): piece = source[entry[0], entry[3]:entry[4]]]
  transfers between devices with their start and end apart: 12 -> 0, of which waited for: 4 -> 0; matrix products, arithmetic and copies ran while one was open for 13% -> 0% of each run, Pallas kernels for 0% -> 0%
where the time goes in v1:
time: 121 us; the launch traced here: 120 us
  Pallas kernels  116 us (96%)
  local copies, waits for them, and re-layouts  3.9 us (3%)
    pallas_call x1, Pallas kernels, shards(): pl.pallas_call(kernel, out_shape=(jax.ShapeDtypeStruct((8, 256, 256), BF1...  116 us
    unnamed x2, local copies, waits for them, and re-layouts  3.9 us

profile of v1, /device:TPU:32, one launch (start us, length us, event | category | flops | bytes accessed | tf_op | source)
XLA Modules:
  0.0 120.4 jit_solution(7427800194860704421)
XLA Ops:
  0.6 115.9 %shard_map.59 = (bf16[8,256,256]{2,1,0:T(8,128)(2,1)}, f32[3,9,8,256]{3,2,1,0:T(8,128)}) custom-call(bf16[2048,256]{1,0:T(8,128)(2,1)} %bitcast.1, bf16[3,8,32,256]{3,2,1,0:T(8,128)(2,1)} %gout.1, bf16[3,8,32,256]{3,2,1,0:T(8,128)(2,1)} %pre.1, bf16[3,9,256,256]{3,2,1,0:T(8,128)(2,1)} %w.1), custom_call_target="tpu_custom_call" | custom-call | flops 14495514624 | bytes 8388608 | tf_op jit(solution)/shard_map/pallas_call | solution.py:336
  116.5 2.3 %copy.8 = bf16[8,256,256]{2,1,0:T(8,128)(2,1)} copy(bf16[8,256,256]{2,1,0:T(8,128)(2,1)} %get-tuple-element.4) | data formatting | bytes 2097152
  118.8 1.6 %copy.9 = f32[3,9,8,256]{3,2,1,0:T(8,128)} copy(f32[3,9,8,256]{3,2,1,0:T(8,128)} %get-tuple-element.5) | data formatting | bytes 442368

commit v2 on v1

--- a/solution.py
+++ b/solution.py
@@ -40,10 +40,10 @@
 
 
 def kernel(
-    feat, gout, pre, w, gin, gw,
-    g, m3, wt, acc, part, r0, qs, ry, sz, rz,
+    feat, gout, pre, w_hbm, gin, gw,
+    w, g, m3, wt, acc, part, r0, qs, ry, sz, rz,
     h_send, h_recv, y_send, y_recv, x_send, x_recv, f_send, f_recv,
-    c_send, c_recv, v_send, v_recv, z_send, z_recv,
+    c_send, c_recv, v_send, v_recv, z_send, z_recv, e_send, e_recv, w_sem,
 ):
     s = lax.axis_index("rows")
     k = lax.axis_index("chan")
@@ -56,12 +56,17 @@
     k_left = lax.rem(k + 6, 8)
     k_right = lax.rem(k + 2, 8)
 
+    w_copy = pltpu.make_async_copy(w_hbm, w, w_sem)
+    w_copy.start()
     barrier = pltpu.get_barrier_semaphore()
 
-    @pl.loop(1, 32)
-    def _(d):
-        pl.semaphore_signal(barrier, inc=1, device_id=(lax.rem(s + d, 32), k), device_id_type=MESH)
-
+    for d in (1, 2, 3, 4, 5):
+        for side in (d, 32 - d):
+            pl.semaphore_signal(barrier, inc=1, device_id=(lax.rem(s + side, 32), k), device_id_type=MESH)
+    for d in range(1, 8):
+        z_peer = yl * 16 + lax.rem(zpos + d, 8) * 2 + core
+        pl.semaphore_signal(barrier, inc=1, device_id=(z_peer, k), device_id_type=MESH)
+    pl.semaphore_signal(barrier, inc=1, device_id=(lax.rem(s + 16, 32), k), device_id_type=MESH)
     for peer in (k_pair, k_left, k_right):
         pl.semaphore_signal(barrier, inc=1, device_id=(s, peer), device_id_type=MESH)
 
@@ -80,7 +85,7 @@
             else:
                 g[p, own, cols] = jnp.zeros((UNIT, rows * COLS), BF16)
 
-    pl.semaphore_wait(barrier, 34)
+    pl.semaphore_wait(barrier, 21)
 
     def halo_copy(n):
         p, offset, there, here, rows = PARTS[n]
@@ -125,8 +130,14 @@
     def pair_rows(first, count=2 * UNIT):
         return pl.ds(pl.multiple_of(first * UNIT, UNIT), count)
 
+    def e_copies():
+        return (
+            remote(g.at[0, own], g.at[0, own], e_send.at[0], e_recv.at[0], (s, k_right)),
+            remote(g.at[0, own], g.at[0, own], e_send.at[1], e_recv.at[1], (s, k_left)),
+        )
+
     def x_copies(p):
-        rows = pair_rows(k_even)
+        rows = pair_rows(k_pair, UNIT) if p == 0 else pair_rows(k_even)
         return (
             remote(g.at[p, rows], g.at[p, rows], x_send.at[p, 0], x_recv.at[p, 0], (s, k_right)),
             remote(g.at[p, rows], g.at[p, rows], x_send.at[p, 1], x_recv.at[p, 1], (s, k_left)),
@@ -151,6 +162,9 @@
             copy.start()
 
     def stage_f(p):
+        if p == 0:
+            for copy in e_copies():
+                copy.wait_recv()
         for copy in x_copies(p):
             copy.wait_recv()
         for copy in f_copies(p):
@@ -187,26 +201,23 @@
         b, i = PIECES[p]
         rate = RATES[b]
 
-        @pl.loop(0, STRIP)
-        def _(y):
-            cols = pl.ds(pl.multiple_of(y * COLS, COLS), COLS)
+        lane = lax.broadcasted_iota(jnp.int32, (1, COLS), 1)
+        keep_lo = (lane >= rate).astype(F32).astype(BF16)
+        keep_hi = (lane < COLS - rate).astype(F32).astype(BF16)
+        for y in range(STRIP):
+            cols = slice(y * COLS, (y + 1) * COLS)
             value = g[p, :, cols]
-            edge = jnp.zeros((256, rate), BF16)
-            m3[0:256, cols] = jnp.concatenate([value[:, rate:], edge], axis=1)
+            m3[0:256, cols] = pltpu.roll(value, COLS - rate, 1) * keep_hi
             m3[256:512, cols] = value
-            m3[512:768, cols] = jnp.concatenate([edge, value[:, : COLS - rate]], axis=1)
-
-        @pl.loop(0, 3)
-        def _(j):
-            rows = pl.ds(pl.multiple_of(j * 256, 256), 256)
-            product = jnp.dot(m3[rows, :], feat[...], preferred_element_type=F32)
-            part[p, j] = product.reshape(2, 8, 2, 8, 256)
+            m3[512:768, cols] = pltpu.roll(value, rate, 1) * keep_lo
+
+        product = jnp.dot(m3[...], feat[...], preferred_element_type=F32)
+        part[p] = product.reshape(3, 2, 8, 2, 8, 256)
 
         c_copy(p).start()
 
-        @pl.loop(0, STRIP)
-        def _(y):
-            cols = pl.ds(pl.multiple_of(y * COLS, COLS), COLS)
+        for h in range(2):
+            cols = slice(h * 1024, (h + 1) * 1024)
             product = jnp.dot(wt[p], m3[:, cols], preferred_element_type=F32)
             if first:
                 acc[:, cols] = product
@@ -235,11 +246,14 @@
         gw[b, 3 * (i + 1) : 3 * (i + 1) + 3] = total * grad_scale
 
     stage_y(0)
+    for copy in e_copies():
+        copy.start()
     for p in (1, 2):
         stage_y(p)
     for p in (5, 6, 7, 8):
         halo_sends(p)
     stage_x(0)
+    w_copy.wait()
     transpose_kernels(0)
     stage_x(1)
     stage_f(0)
@@ -254,54 +268,53 @@
     compute(0, True)
     stage_x(5)
     transpose_kernels(2)
+    reduce_core(0)
     stage_ready(1)
     stage_f(2)
     stage_y(7)
     compute(1, False)
-    reduce_core(0)
     stage_x(6)
     transpose_kernels(3)
+    reduce_core(1)
+    reduce_y(0)
     stage_ready(2)
     stage_f(5)
     stage_y(8)
     compute(2, False)
-    reduce_core(1)
-    reduce_y(0)
     stage_x(7)
+    transpose_kernels(4)
+    reduce_core(2)
+    reduce_y(1)
+    stage_ready(3)
+    compute(3, False)
     transpose_kernels(5)
     stage_ready(5)
     stage_f(6)
     compute(5, False)
-    reduce_core(2)
-    reduce_y(1)
     stage_x(8)
-    transpose_kernels(4)
-    stage_ready(3)
-    compute(3, False)
+    reduce_core(3)
+    reduce_y(2)
+    stage_ready(4)
+    compute(4, False)
+    transpose_kernels(6)
     reduce_core(5)
-    reduce_y(2)
-    transpose_kernels(6)
+    reduce_y(3)
     stage_ready(6)
     stage_f(7)
     compute(6, False)
-    reduce_core(3)
+    reduce_core(4)
     reduce_y(5)
-    stage_ready(4)
-    compute(4, False)
-    reduce_core(6)
-    reduce_y(3)
     transpose_kernels(7)
     transpose_kernels(8)
-    reduce_z(0)
     stage_ready(7)
     stage_f(8)
     compute(7, False)
-    reduce_core(4)
+    reduce_core(6)
+    reduce_y(4)
+    reduce_core(7)
     reduce_y(6)
-    reduce_z(1)
-    reduce_z(2)
-    reduce_core(7)
-    reduce_y(4)
+    for p in (0, 1, 2, 3):
+        reduce_z(p)
     stage_ready(8)
     compute(8, False)
     reduce_y(7)
@@ -313,9 +326,11 @@
         gin[y] = acc[:, cols].astype(BF16).T
 
     reduce_y(8)
-    for p in (5, 3, 6, 4, 7, 8):
+    for p in (5, 4, 6, 7, 8):
         reduce_z(p)
 
+    for copy in e_copies():
+        copy.wait_send()
     for p in range(9):
         if PIECES[p][1] != 0:
             halo_drain(p)
@@ -339,9 +354,10 @@
             jax.ShapeDtypeStruct((8, 256, 256), BF16),
             jax.ShapeDtypeStruct((3, 9, 8, 256), F32),
         ),
-        in_specs=[vmem] * 4,
+        in_specs=[vmem] * 3 + [pl.BlockSpec(memory_space=pl.ANY)],
         out_specs=(vmem, vmem),
         scratch_shapes=[
+            pltpu.VMEM((3, 9, 256, 256), BF16),
             pltpu.VMEM((9, 256, 2048), BF16),
             pltpu.VMEM((768, 2048), BF16),
             pltpu.VMEM((9, 256, 768), BF16),
@@ -359,6 +375,8 @@
             dma((9,)), dma((9,)),
             dma((9,)), dma((9,)),
             dma((9,)), dma((9,)),
+            dma((2,)), dma((2,)),
+            pltpu.SemaphoreType.DMA,
         ],
         compiler_params=pltpu.CompilerParams(
             collective_id=0, has_side_effects=True, vmem_limit_bytes=62 * 2**20

time: 121 us -> 111 us (0.917)
  Pallas kernels: 116 us -> 106 us
    pallas_call x1, Pallas kernels: 116 us -> 106 us  [shards(): pl.pallas_call(kernel, out_shape=(jax.ShapeDtypeStruct((8, 256, 256), BF1...]
where the time goes in v2:
time: 111 us
  Pallas kernels  106 us (95%)
  local copies, waits for them, and re-layouts  3.9 us (4%)
    pallas_call x1, Pallas kernels, shards(): pl.pallas_call(kernel, out_shape=(jax.ShapeDtypeStruct((8, 256, 256), BF1...  106 us
    unnamed x2, local copies, waits for them, and re-layouts  3.9 us

profile of v2, /device:TPU:32, one launch (start us, length us, event | category | flops | bytes accessed | tf_op | source)
XLA Modules:
  0.0 110.7 jit_solution(5284592183170853192)
XLA Ops:
  0.6 106.2 %shard_map.59 = (bf16[8,256,256]{2,1,0:T(8,128)(2,1)}, f32[3,9,8,256]{3,2,1,0:T(8,128)}) custom-call(bf16[2048,256]{1,0:T(8,128)(2,1)} %bitcast.1, bf16[3,8,32,256]{3,2,1,0:T(8,128)(2,1)} %gout.1, bf16[3,8,32,256]{3,2,1,0:T(8,128)(2,1)} %pre.1, bf16[3,9,256,256]{3,2,1,0:T(8,128)(2,1)} %w_hbm.1), custom_call_target="tpu_custom_call" | custom-call | flops 14495514624 | bytes 8388608 | tf_op jit(solution)/shard_map/pallas_call | solution.py:351
  106.8 2.3 %copy.8 = bf16[8,256,256]{2,1,0:T(8,128)(2,1)} copy(bf16[8,256,256]{2,1,0:T(8,128)(2,1)} %get-tuple-element.4) | data formatting | bytes 2097152
  109.1 1.6 %copy.9 = f32[3,9,8,256]{3,2,1,0:T(8,128)} copy(f32[3,9,8,256]{3,2,1,0:T(8,128)} %get-tuple-element.5) | data formatting | bytes 442368

commit v3 on v2

--- a/solution.py
+++ b/solution.py
@@ -18,7 +18,20 @@
 
 STRIP = 8
 COLS = 256
+SPLIT = (8,)
 UNIT = 32
+
+
+ORDER = (
+    "y0", "e0", "y1", "y2", "h5", "h6", "h7", "h8", "x0", "w0", "t0", "x1",
+    "f0", "y5", "x2", "t1", "r0", "h3", "h4", "f1", "y6", "k0", "I0", "x5",
+    "t2", "c0", "r1", "f2", "y7", "k1", "i1", "x6", "t3", "c1", "r2", "f5",
+    "y8", "k2", "i2", "x7", "t4", "c2", "v0", "r3", "k3", "i3", "t5", "r5",
+    "f6", "k5", "i5", "x8", "c3", "v1", "r4", "k4", "i4", "t6", "c5", "v2",
+    "r6", "f7", "k6", "i6", "c4", "v3", "t7", "t8", "r7", "f8", "k7", "i7",
+    "v5", "c6", "c7", "v4", "z0", "z1", "r8", "k8", "C8", "v6", "v7", "i8",
+    "V8", "o0", "z2", "z3", "z5", "z4", "z6", "z7", "z8",
+)
 
 
 def row_parts():
@@ -37,6 +50,10 @@
 
 
 PARTS = row_parts()
+
+
+def chunks(p):
+    return (0, 1, 2) if p in SPLIT else (None,)
 
 
 def kernel(
@@ -182,22 +199,35 @@
         for j in range(3):
             wt[p, :, j * 256 : (j + 1) * 256] = w[b, (i + 1) * 3 + j].T
 
-    def c_copy(p):
-        return remote(part.at[p, :, :, :, 1 - core], r0.at[p], c_send.at[p], c_recv.at[p], (s + 1 - 2 * core, k))
-
-    def v_copy(p):
-        return remote(qs.at[p], ry.at[p], v_send.at[p], v_recv.at[p], (lax.rem(s + 16, 32), k))
-
-    def z_copy(p, d):
+    def slot(p, j):
+        return p if j is None else p + j
+
+    def c_copy(p, j=None):
+        src, dst = (part.at[p], r0.at[p]) if j is None else (part.at[p, j : j + 1], r0.at[p, j : j + 1])
+        n = slot(p, j)
+        return remote(src.at[:, :, :, 1 - core], dst, c_send.at[n], c_recv.at[n], (s + 1 - 2 * core, k))
+
+    def v_copy(p, j=None):
+        src, dst = (qs.at[p], ry.at[p]) if j is None else (qs.at[p, j], ry.at[p, j])
+        n = slot(p, j)
+        return remote(src, dst, v_send.at[n], v_recv.at[n], (lax.rem(s + 16, 32), k))
+
+    def z_copy(p, d, j=None):
         z_to = lax.rem(zpos + d, 8)
-        return remote(
-            sz.at[p, z_to], rz.at[p, d - 1], z_send.at[p], z_recv.at[p], (yl * 16 + z_to * 2 + core, k)
-        )
-
-    def z_whole(p):
-        return remote(sz.at[p, 0:7], rz.at[p], z_send.at[p], z_recv.at[p], (lax.rem(s + 2, 32), k))
-
-    def compute(p, first):
+        src, dst = sz.at[p, z_to], rz.at[p, d - 1]
+        if j is not None:
+            src, dst = src.at[j], dst.at[j]
+        n = slot(p, j)
+        return remote(src, dst, z_send.at[n], z_recv.at[n], (yl * 16 + z_to * 2 + core, k))
+
+    def z_whole(p, j=None):
+        src, dst = sz.at[p, 0:7], rz.at[p]
+        if j is not None:
+            src, dst = src.at[:, j], dst.at[:, j]
+        n = slot(p, j)
+        return remote(src, dst, z_send.at[n], z_recv.at[n], (lax.rem(s + 2, 32), k))
+
+    def compute_kernels(p):
         b, i = PIECES[p]
         rate = RATES[b]
 
@@ -211,11 +241,17 @@
             m3[256:512, cols] = value
             m3[512:768, cols] = pltpu.roll(value, rate, 1) * keep_lo
 
-        product = jnp.dot(m3[...], feat[...], preferred_element_type=F32)
-        part[p] = product.reshape(3, 2, 8, 2, 8, 256)
-
-        c_copy(p).start()
-
+        if p in SPLIT:
+            for j in range(3):
+                product = jnp.dot(m3[j * 256 : (j + 1) * 256, :], feat[...], preferred_element_type=F32)
+                part[p, j] = product.reshape(2, 8, 2, 8, 256)
+                c_copy(p, j).start()
+        else:
+            product = jnp.dot(m3[...], feat[...], preferred_element_type=F32)
+            part[p] = product.reshape(3, 2, 8, 2, 8, 256)
+            c_copy(p).start()
+
+    def compute_input(p, first=False):
         for h in range(2):
             cols = slice(h * 1024, (h + 1) * 1024)
             product = jnp.dot(wt[p], m3[:, cols], preferred_element_type=F32)
@@ -224,110 +260,59 @@
             else:
                 acc[:, cols] += product
 
-    def reduce_core(p):
-        c_copy(p).wait_recv()
-        for j in range(3):
+    def compute(p, first=False):
+        compute_kernels(p)
+        compute_input(p, first)
+
+    def reduce_core(p, only=None):
+        c_copy(p, only).wait_recv()
+        for j in range(3) if only is None else (only,):
             qs[p, j] = part[p, j, 1 - yl, :, core] + r0[p, j, 1 - yl]
-        v_copy(p).start()
-
-    def reduce_y(p):
-        v_copy(p).wait_recv()
-        for j in range(3):
+        v_copy(p, only).start()
+
+    def reduce_y(p, only=None):
+        v_copy(p, only).wait_recv()
+        for j in range(3) if only is None else (only,):
             sz[p, :, j] = part[p, j, yl, :, core] + r0[p, j, yl] + ry[p, j]
         for d in range(1, 8):
-            z_copy(p, d).start()
+            z_copy(p, d, only).start()
 
     def reduce_z(p):
         b, i = PIECES[p]
-        z_whole(p).wait_recv()
+        for only in chunks(p):
+            z_whole(p, only).wait_recv()
         total = sz[p, zpos]
         for d in range(7):
             total = total + rz[p, d]
         gw[b, 3 * (i + 1) : 3 * (i + 1) + 3] = total * grad_scale
 
-    stage_y(0)
-    for copy in e_copies():
-        copy.start()
-    for p in (1, 2):
-        stage_y(p)
-    for p in (5, 6, 7, 8):
-        halo_sends(p)
-    stage_x(0)
-    w_copy.wait()
-    transpose_kernels(0)
-    stage_x(1)
-    stage_f(0)
-    stage_y(5)
-    stage_x(2)
-    transpose_kernels(1)
-    stage_ready(0)
-    for p in DIRECT:
-        halo_sends(p)
-    stage_f(1)
-    stage_y(6)
-    compute(0, True)
-    stage_x(5)
-    transpose_kernels(2)
-    reduce_core(0)
-    stage_ready(1)
-    stage_f(2)
-    stage_y(7)
-    compute(1, False)
-    stage_x(6)
-    transpose_kernels(3)
-    reduce_core(1)
-    reduce_y(0)
-    stage_ready(2)
-    stage_f(5)
-    stage_y(8)
-    compute(2, False)
-    stage_x(7)
-    transpose_kernels(4)
-    reduce_core(2)
-    reduce_y(1)
-    stage_ready(3)
-    compute(3, False)
-    transpose_kernels(5)
-    stage_ready(5)
-    stage_f(6)
-    compute(5, False)
-    stage_x(8)
-    reduce_core(3)
-    reduce_y(2)
-    stage_ready(4)
-    compute(4, False)
-    transpose_kernels(6)
-    reduce_core(5)
-    reduce_y(3)
-    stage_ready(6)
-    stage_f(7)
-    compute(6, False)
-    reduce_core(4)
-    reduce_y(5)
-    transpose_kernels(7)
-    transpose_kernels(8)
-    stage_ready(7)
-    stage_f(8)
-    compute(7, False)
-    reduce_core(6)
-    reduce_y(4)
-    reduce_core(7)
-    reduce_y(6)
-    for p in (0, 1, 2, 3):
-        reduce_z(p)
-    stage_ready(8)
-    compute(8, False)
-    reduce_y(7)
-    reduce_core(8)
-
-    @pl.loop(0, STRIP)
-    def _(y):
-        cols = pl.ds(pl.multiple_of(y * COLS, COLS), COLS)
-        gin[y] = acc[:, cols].astype(BF16).T
-
-    reduce_y(8)
-    for p in (5, 4, 6, 7, 8):
-        reduce_z(p)
+    def own_first(_):
+        for copy in e_copies():
+            copy.start()
+
+    def weights_in(_):
+        w_copy.wait()
+
+    def split_core(p):
+        for j in range(3):
+            reduce_core(p, j)
+
+    def split_y(p):
+        for j in range(3):
+            reduce_y(p, j)
+
+    def write_input(_):
+        for y in range(STRIP):
+            gin[y] = acc[:, y * COLS : (y + 1) * COLS].astype(BF16).T
+
+    steps = {
+        "e": own_first, "y": stage_y, "h": halo_sends, "x": stage_x, "f": stage_f, "r": stage_ready,
+        "w": weights_in, "t": transpose_kernels, "k": compute_kernels, "i": compute_input,
+        "I": lambda p: compute_input(p, True), "c": reduce_core, "v": reduce_y, "z": reduce_z,
+        "C": split_core, "V": split_y, "o": write_input,
+    }
+    for step in ORDER:
+        steps[step[0]](int(step[1]))
 
     for copy in e_copies():
         copy.wait_send()
@@ -340,9 +325,10 @@
                 copy.wait_send()
             for copy in f_copies(p):
                 copy.wait_send()
-        c_copy(p).wait_send()
-        v_copy(p).wait_send()
-        z_whole(p).wait_send()
+        for j in chunks(p):
+            c_copy(p, j).wait_send()
+            v_copy(p, j).wait_send()
+            z_whole(p, j).wait_send()
 
 
 def shards(features, grad_out, pre_act, weights):
@@ -372,9 +358,9 @@
             dma((9,)), dma((9,)),
             dma((9, 2)), dma((9, 2)),
             dma((9, 2)), dma((9, 2)),
-            dma((9,)), dma((9,)),
-            dma((9,)), dma((9,)),
-            dma((9,)), dma((9,)),
+            dma((11,)), dma((11,)),
+            dma((11,)), dma((11,)),
+            dma((11,)), dma((11,)),
             dma((2,)), dma((2,)),
             pltpu.SemaphoreType.DMA,
         ],

time: 111 us -> 109 us (0.982)
    pallas_call x1, Pallas kernels: 106 us -> 105 us  [shards(): pl.pallas_call(kernel, out_shape=(jax.ShapeDtypeStruct((8, 256, 256), BF1...]
where the time goes in v3:
time: 109 us
  Pallas kernels  105 us (96%)
  local copies, waits for them, and re-layouts  3.9 us (4%)
    pallas_call x1, Pallas kernels, shards(): pl.pallas_call(kernel, out_shape=(jax.ShapeDtypeStruct((8, 256, 256), BF1...  105 us
    unnamed x2, local copies, waits for them, and re-layouts  3.9 us

profile of v3, /device:TPU:32, one launch (start us, length us, event | category | flops | bytes accessed | tf_op | source)
XLA Modules:
  0.0 109.2 jit_solution(16286692367302974499)
XLA Ops:
  0.6 104.7 %shard_map.59 = (bf16[8,256,256]{2,1,0:T(8,128)(2,1)}, f32[3,9,8,256]{3,2,1,0:T(8,128)}) custom-call(bf16[2048,256]{1,0:T(8,128)(2,1)} %bitcast.1, bf16[3,8,32,256]{3,2,1,0:T(8,128)(2,1)} %gout.1, bf16[3,8,32,256]{3,2,1,0:T(8,128)(2,1)} %pre.1, bf16[3,9,256,256]{3,2,1,0:T(8,128)(2,1)} %w_hbm.1), custom_call_target="tpu_custom_call" | custom-call | flops 14495514624 | bytes 8388608 | tf_op jit(solution)/shard_map/pallas_call | solution.py:337
  105.3 2.3 %copy.8 = bf16[8,256,256]{2,1,0:T(8,128)(2,1)} copy(bf16[8,256,256]{2,1,0:T(8,128)(2,1)} %get-tuple-element.4) | data formatting | bytes 2097152
  107.6 1.6 %copy.9 = f32[3,9,8,256]{3,2,1,0:T(8,128)} copy(f32[3,9,8,256]{3,2,1,0:T(8,128)} %get-tuple-element.5) | data formatting | bytes 442368

commit v4 on v3

--- a/solution.py
+++ b/solution.py
@@ -57,10 +57,10 @@
 
 
 def kernel(
-    feat, gout, pre, w_hbm, gin, gw,
-    w, g, m3, wt, acc, part, r0, qs, ry, sz, rz,
+    feat_hbm, gout, pre, w_hbm, gin, gw,
+    feat, w, g, m3, wt, acc, part, r0, qs, ry, sz, rz,
     h_send, h_recv, y_send, y_recv, x_send, x_recv, f_send, f_recv,
-    c_send, c_recv, v_send, v_recv, z_send, z_recv, e_send, e_recv, w_sem,
+    c_send, c_recv, v_send, v_recv, z_send, z_recv, e_send, e_recv, w_sem, feat_sem,
 ):
     s = lax.axis_index("rows")
     k = lax.axis_index("chan")
@@ -75,6 +75,8 @@
 
     w_copy = pltpu.make_async_copy(w_hbm, w, w_sem)
     w_copy.start()
+    feat_copy = pltpu.make_async_copy(feat_hbm, feat, feat_sem)
+    feat_copy.start()
     barrier = pltpu.get_barrier_semaphore()
 
     for d in (1, 2, 3, 4, 5):
@@ -292,6 +294,7 @@
 
     def weights_in(_):
         w_copy.wait()
+        feat_copy.wait()
 
     def split_core(p):
         for j in range(3):
@@ -340,9 +343,10 @@
             jax.ShapeDtypeStruct((8, 256, 256), BF16),
             jax.ShapeDtypeStruct((3, 9, 8, 256), F32),
         ),
-        in_specs=[vmem] * 3 + [pl.BlockSpec(memory_space=pl.ANY)],
+        in_specs=[pl.BlockSpec(memory_space=pl.ANY), vmem, vmem, pl.BlockSpec(memory_space=pl.ANY)],
         out_specs=(vmem, vmem),
         scratch_shapes=[
+            pltpu.VMEM((2048, 256), BF16),
             pltpu.VMEM((3, 9, 256, 256), BF16),
             pltpu.VMEM((9, 256, 2048), BF16),
             pltpu.VMEM((768, 2048), BF16),
@@ -363,6 +367,7 @@
             dma((11,)), dma((11,)),
             dma((2,)), dma((2,)),
             pltpu.SemaphoreType.DMA,
+            pltpu.SemaphoreType.DMA,
         ],
         compiler_params=pltpu.CompilerParams(
             collective_id=0, has_side_effects=True, vmem_limit_bytes=62 * 2**20

time: 109 us -> 109 us (level)
  no operation moved by 1% of the time
where the time goes in v4:
time: 109 us; the launch traced here: 108 us
  Pallas kernels  104 us (95%)
  local copies, waits for them, and re-layouts  3.9 us (4%)
    pallas_call x1, Pallas kernels, shards(): pl.pallas_call(kernel, out_shape=(jax.ShapeDtypeStruct((8, 256, 256), BF1...  104 us
    unnamed x2, local copies, waits for them, and re-layouts  3.9 us

profile of v4, /device:TPU:32, one launch (start us, length us, event | category | flops | bytes accessed | tf_op | source)
XLA Modules:
  0.0 108.3 jit_solution(8147379700558064162)
XLA Ops:
  0.6 103.8 %shard_map.59 = (bf16[8,256,256]{2,1,0:T(8,128)(2,1)}, f32[3,9,8,256]{3,2,1,0:T(8,128)}) custom-call(bf16[2048,256]{1,0:T(8,128)(2,1)} %bitcast.1, bf16[3,8,32,256]{3,2,1,0:T(8,128)(2,1)} %gout.1, bf16[3,8,32,256]{3,2,1,0:T(8,128)(2,1)} %pre.1, bf16[3,9,256,256]{3,2,1,0:T(8,128)(2,1)} %w_hbm.1), custom_call_target="tpu_custom_call" | custom-call | flops 14495514624 | bytes 8388608 | tf_op jit(solution)/shard_map/pallas_call | solution.py:340
  104.4 2.3 %copy.8 = bf16[8,256,256]{2,1,0:T(8,128)(2,1)} copy(bf16[8,256,256]{2,1,0:T(8,128)(2,1)} %get-tuple-element.4) | data formatting | bytes 2097152
  106.7 1.6 %copy.9 = f32[3,9,8,256]{3,2,1,0:T(8,128)} copy(f32[3,9,8,256]{3,2,1,0:T(8,128)} %get-tuple-element.5) | data formatting | bytes 442368
